TPU v7x, 32 devices: a whole 2x2x4 slice. The times are simulated.
32 devices in a mesh: ctx: 8 (over y, x, core), fsdp: 4 (over z).
Axes of the slice: x: 2, y: 2, z: 4, core: 2. Of those that a mesh axis runs over, the one named last changes fastest.
Arguments:
- pixels: bfloat16 [4, 8192, 261], P('fsdp', 'ctx'), may hold values from -8 to 8
- latents: bfloat16 [4, 1024, 1024], P('fsdp', 'ctx'), may hold values from -6 to 6
- cotangent: bfloat16 [4, 1024, 1024], P('fsdp', 'ctx'), may hold values from -6 to 6
- doc_lengths: int32 [4, 4], P('fsdp'), may hold values from 1 to 6144, 8192 in all within a row
- latent_offsets: int32 [4, 1024], P('fsdp'), may hold values from 0 to 7
- block_deal: int32 [16], replicated, may hold values from 0 to 15, each once
- query_cross: float32 [1024, 1024], P('fsdp'), may hold values from -0.1875 to 0.1875
- key_cross: float32 [261, 1024], P(None, 'fsdp'), may hold values from -0.375 to 0.375
- value_cross: float32 [261, 1024], P(None, 'fsdp'), may hold values from -0.375 to 0.375
- out_cross: float32 [1024, 1024], P('fsdp'), may hold values from -3 to 3
- up_cross: float32 [1024, 1024], P('fsdp'), may hold values from -0.1875 to 0.1875
- down_cross: float32 [1024, 1024], P('fsdp'), may hold values from -0.1875 to 0.1875
- query_self: float32 [1024, 1024], P('fsdp'), may hold values from -0.1875 to 0.1875
- key_self: float32 [1024, 1024], P('fsdp'), may hold values from -0.1875 to 0.1875
- value_self: float32 [1024, 1024], P('fsdp'), may hold values from -0.1875 to 0.1875
- out_self: float32 [1024, 1024], P('fsdp'), may hold values from -3 to 3
- up_self: float32 [1024, 1024], P('fsdp'), may hold values from -0.1875 to 0.1875
- down_self: float32 [1024, 1024], P('fsdp'), may hold values from -0.1875 to 0.1875
- gain_input: float32 [261], replicated, may hold values from 0.1 to 1.9
- gain_latent: float32 [1024], replicated, may hold values from 0.1 to 1.9
- gain_cross_mlp: float32 [1024], replicated, may hold values from 0.1 to 1.9
- gain_self: float32 [1024], replicated, may hold values from 0.1 to 1.9
- gain_self_mlp: float32 [1024], replicated, may hold values from 0.1 to 1.9
Outputs:
- layer_out: bfloat16 [4, 1024, 1024], P('fsdp', 'ctx')
- grad_pixels: float32 [4, 8192, 261], P('fsdp', 'ctx')
- grad_latents: float32 [4, 1024, 1024], P('fsdp', 'ctx')
- grad_query_cross: float32 [1024, 1024], P('fsdp')
- grad_key_cross: float32 [261, 1024], P(None, 'fsdp')
- grad_value_cross: float32 [261, 1024], P(None, 'fsdp')
- grad_out_cross: float32 [1024, 1024], P('fsdp')
- grad_up_cross: float32 [1024, 1024], P('fsdp')
- grad_down_cross: float32 [1024, 1024], P('fsdp')
- grad_query_self: float32 [1024, 1024], P('fsdp')
- grad_key_self: float32 [1024, 1024], P('fsdp')
- grad_value_self: float32 [1024, 1024], P('fsdp')
- grad_out_self: float32 [1024, 1024], P('fsdp')
- grad_up_self: float32 [1024, 1024], P('fsdp')
- grad_down_self: float32 [1024, 1024], P('fsdp')
- grad_gain_input: float32 [261], replicated
- grad_gain_latent: float32 [1024], replicated
- grad_gain_cross_mlp: float32 [1024], replicated
- grad_gain_self: float32 [1024], replicated
- grad_gain_self_mlp: float32 [1024], replicated
Inputs may be any that keep to these rules, and one draw needn't show every extreme that they name: `doc_lengths`: each row holds the lengths of 4 documents that together fill the 8192 pixel rows of its sequence; one is exactly 6144 long. `block_deal`: a permutation of the 16 latent blocks.
All inputs are finite; a program needn't handle non-finite values.
Results may differ from a plain program's by a relative error of at most 0.028.
Values may be sent and summed in bfloat16 or wider, within the bound.
A program may use at most 320 MiB of HBM per device.

v0:
```python
import math

import jax
import jax.numpy as jnp
from jax import lax
from jax.sharding import PartitionSpec as P

D = 1024
HEADS = 8
PIX_DEV = 1024
STRIDE = 8
LAT_DEV = 128
LBLK = 64


masked_fill = -1e30


def joined(part, axis, combine):
    gathered = jax.tree.map(lambda a: lax.all_gather(a, axis), part)

    def take(source):
        return jax.tree.map(lambda a: lax.dynamic_index_in_dim(a, source, 0, False), gathered)

    return lax.fori_loop(
        1, lax.axis_size(axis), lambda source, state: combine(state, take(source)), take(0)
    )


def matmul(inputs, weight):
    return jnp.dot(inputs, weight, preferred_element_type=jnp.float32)


def transposed(grad_rows, matrix):
    return jnp.einsum("rd,fd->rf", grad_rows, matrix, preferred_element_type=jnp.float32)


def outer_sum(inputs, grad_rows):
    return jnp.einsum("ri,ro->io", inputs, grad_rows, preferred_element_type=jnp.float32)


def layer_norm(values, gain):
    center = values - jnp.mean(values, axis=-1, keepdims=True)
    spread = jnp.mean(center * center, axis=-1, keepdims=True)
    return center * lax.rsqrt(spread + 1e-05) * gain


def doc_index(positions, starts):
    return jnp.sum((positions[:, None] >= starts[None, :]).astype(jnp.int32), axis=1) - 1


def latent_positions(block_deal, offsets):
    base = (block_deal[:, None] * LBLK + jnp.arange(LBLK, dtype=jnp.int32)[None, :]).reshape(-1)
    return base * STRIDE + offsets


def combine_stats(earlier, later):
    top_one, total_one = earlier
    top_two, total_two = later
    highest = jnp.maximum(top_one, top_two)
    return (
        highest,
        total_one * jnp.exp(top_one - highest) + total_two * jnp.exp(top_two - highest),
    )


def mlp_back(upstream, residual, gain, normed, hidden, active, up_full, down_full):
    grad_low = upstream.astype(jnp.bfloat16)
    grad_down = outer_sum(active, grad_low)
    gelu_out, gelu_pull = jax.vjp(jax.nn.gelu, hidden)
    grad_hidden = gelu_pull(transposed(grad_low, down_full))[0].astype(jnp.bfloat16)
    grad_up = outer_sum(normed, grad_hidden)
    norm_out, norm_pull = jax.vjp(layer_norm, residual, gain)
    grad_res, grad_gain = norm_pull(transposed(grad_hidden, up_full))
    return (upstream + grad_res, grad_up, grad_down, grad_gain)


def local(
    pixels,
    latents,
    cotangent,
    doc_lengths,
    latent_offsets,
    block_deal,
    query_cross,
    key_cross,
    value_cross,
    out_cross,
    up_cross,
    down_cross,
    query_self,
    key_self,
    value_self,
    out_self,
    up_self,
    down_self,
    gain_input,
    gain_latent,
    gain_cross_mlp,
    gain_self,
    gain_self_mlp,
):
    ctx_count = lax.axis_size("ctx")
    ctx_place = lax.axis_index("ctx")
    lat_count = LAT_DEV * ctx_count
    head_dim = D // HEADS
    cross_scale = 1.0 / math.sqrt(D)
    self_scale = 1.0 / math.sqrt(head_dim)
    lengths = doc_lengths[0]
    starts = jnp.cumsum(lengths) - lengths
    lat_pos = latent_positions(block_deal, latent_offsets[0])
    lat_doc = doc_index(lat_pos, starts)
    own_pos = lax.dynamic_slice_in_dim(lat_pos, ctx_place * LAT_DEV, LAT_DEV)
    own_doc = lax.dynamic_slice_in_dim(lat_doc, ctx_place * LAT_DEV, LAT_DEV)
    pix_pos = ctx_place * PIX_DEV + jnp.arange(PIX_DEV, dtype=jnp.int32)
    pix_doc = doc_index(pix_pos, starts)
    cross_mask = (lat_doc[:, None] == pix_doc[None, :]) & (pix_pos[None, :] <= lat_pos[:, None])
    self_mask = (own_doc[:, None] == lat_doc[None, :]) & (lat_pos[None, :] <= own_pos[:, None])
    weights = (
        lax.all_gather(query_cross.astype(jnp.bfloat16), "fsdp", axis=0, tiled=True),
        lax.all_gather(key_cross.astype(jnp.bfloat16), "fsdp", axis=1, tiled=True),
        lax.all_gather(value_cross.astype(jnp.bfloat16), "fsdp", axis=1, tiled=True),
        lax.all_gather(out_cross.astype(jnp.bfloat16), "fsdp", axis=0, tiled=True),
        lax.all_gather(up_cross.astype(jnp.bfloat16), "fsdp", axis=0, tiled=True),
        lax.all_gather(down_cross.astype(jnp.bfloat16), "fsdp", axis=0, tiled=True),
        lax.all_gather(query_self.astype(jnp.bfloat16), "fsdp", axis=0, tiled=True),
        lax.all_gather(key_self.astype(jnp.bfloat16), "fsdp", axis=0, tiled=True),
        lax.all_gather(value_self.astype(jnp.bfloat16), "fsdp", axis=0, tiled=True),
        lax.all_gather(out_self.astype(jnp.bfloat16), "fsdp", axis=0, tiled=True),
        lax.all_gather(up_self.astype(jnp.bfloat16), "fsdp", axis=0, tiled=True),
        lax.all_gather(down_self.astype(jnp.bfloat16), "fsdp", axis=0, tiled=True),
    )
    pix_in = pixels[0].astype(jnp.float32)
    lat_in = latents[0].astype(jnp.float32)
    normed_pix = layer_norm(pix_in, gain_input).astype(jnp.bfloat16)
    keys_cross = matmul(normed_pix, weights[1]).astype(jnp.bfloat16)
    values_cross = matmul(normed_pix, weights[2]).astype(jnp.bfloat16)
    normed_lat = layer_norm(lat_in, gain_latent).astype(jnp.bfloat16)
    queries = matmul(normed_lat, weights[0]).astype(jnp.bfloat16)
    queries_all = lax.all_gather(queries, "ctx", axis=0, tiled=True)

    def cross_scores(query_rows):
        raw_scores = jnp.einsum(
            "qd,kd->qk", query_rows, keys_cross, preferred_element_type=jnp.float32
        )
        return jnp.where(cross_mask, raw_scores * cross_scale, masked_fill)

    scores = cross_scores(queries_all)
    local_max = jnp.max(scores, axis=1)
    local_total = jnp.sum(jnp.where(cross_mask, jnp.exp(scores - local_max[:, None]), 0.0), axis=1)
    row_max, row_total = joined((local_max, local_total), "ctx", combine_stats)

    def recompute_probs(score_rows):
        return jnp.where(
            cross_mask, jnp.exp(score_rows - row_max[:, None]) / row_total[:, None], 0.0
        )

    attention = recompute_probs(scores)
    attention_low = attention.astype(jnp.bfloat16)
    attended = lax.psum_scatter(
        matmul(attention_low, values_cross), "ctx", scatter_dimension=0, tiled=True
    ).astype(jnp.bfloat16)
    residual_one = lat_in + matmul(attended, weights[3])
    normed_one = layer_norm(residual_one, gain_cross_mlp).astype(jnp.bfloat16)
    hidden_one = matmul(normed_one, weights[4])
    active_one = jax.nn.gelu(hidden_one).astype(jnp.bfloat16)
    residual_two = residual_one + matmul(active_one, weights[5])
    normed_two = layer_norm(residual_two, gain_self).astype(jnp.bfloat16)
    self_queries = (
        matmul(normed_two, weights[6]).astype(jnp.bfloat16).reshape(LAT_DEV, HEADS, head_dim)
    )
    self_keys = matmul(normed_two, weights[7]).astype(jnp.bfloat16)
    self_values = matmul(normed_two, weights[8]).astype(jnp.bfloat16)
    keys_all, values_all = (
        lax.all_gather(self_keys, "ctx", axis=0, tiled=True),
        lax.all_gather(self_values, "ctx", axis=0, tiled=True),
    )
    keys_heads = keys_all.reshape(lat_count, HEADS, head_dim)
    values_heads = values_all.reshape(lat_count, HEADS, head_dim)
    self_raw = jnp.einsum(
        "qhd,khd->hqk", self_queries, keys_heads, preferred_element_type=jnp.float32
    )
    self_scores = jnp.where(self_mask[None], self_raw * self_scale, masked_fill)
    self_top = jnp.max(self_scores, axis=-1)
    self_exp = jnp.exp(self_scores - self_top[:, :, None])
    self_sum = jnp.sum(self_exp, axis=-1)
    self_probs = self_exp / self_sum[:, :, None]
    self_low = self_probs.astype(jnp.bfloat16)
    self_joined = jnp.einsum(
        "hqk,khd->qhd", self_low, values_heads, preferred_element_type=jnp.float32
    )
    self_attended = self_joined.reshape(LAT_DEV, D).astype(jnp.bfloat16)
    residual_three = residual_two + matmul(self_attended, weights[9])
    normed_three = layer_norm(residual_three, gain_self_mlp).astype(jnp.bfloat16)
    hidden_three = matmul(normed_three, weights[10])
    active_three = jax.nn.gelu(hidden_three).astype(jnp.bfloat16)
    residual_four = residual_three + matmul(active_three, weights[11])
    layer_out = residual_four.astype(jnp.bfloat16)[None]
    back_weights = (
        lax.all_gather(query_cross.astype(jnp.bfloat16), "fsdp", axis=0, tiled=True),
        lax.all_gather(key_cross.astype(jnp.bfloat16), "fsdp", axis=1, tiled=True),
        lax.all_gather(value_cross.astype(jnp.bfloat16), "fsdp", axis=1, tiled=True),
        lax.all_gather(out_cross.astype(jnp.bfloat16), "fsdp", axis=0, tiled=True),
        lax.all_gather(up_cross.astype(jnp.bfloat16), "fsdp", axis=0, tiled=True),
        lax.all_gather(down_cross.astype(jnp.bfloat16), "fsdp", axis=0, tiled=True),
        lax.all_gather(query_self.astype(jnp.bfloat16), "fsdp", axis=0, tiled=True),
        lax.all_gather(key_self.astype(jnp.bfloat16), "fsdp", axis=0, tiled=True),
        lax.all_gather(value_self.astype(jnp.bfloat16), "fsdp", axis=0, tiled=True),
        lax.all_gather(out_self.astype(jnp.bfloat16), "fsdp", axis=0, tiled=True),
        lax.all_gather(up_self.astype(jnp.bfloat16), "fsdp", axis=0, tiled=True),
        lax.all_gather(down_self.astype(jnp.bfloat16), "fsdp", axis=0, tiled=True),
    )
    upstream = cotangent[0].astype(jnp.float32)
    grad_three, grad_up_self, grad_down_self, grad_gain_self_mlp = mlp_back(
        upstream,
        residual_three,
        gain_self_mlp,
        normed_three,
        hidden_three,
        active_three,
        back_weights[10],
        back_weights[11],
    )
    grad_proj_low = grad_three.astype(jnp.bfloat16)
    grad_out_self = outer_sum(self_attended, grad_proj_low)
    grad_heads = (
        transposed(grad_proj_low, back_weights[9])
        .astype(jnp.bfloat16)
        .reshape(LAT_DEV, HEADS, head_dim)
    )
    grad_self_probs = jnp.einsum(
        "qhd,khd->hqk", grad_heads, values_heads, preferred_element_type=jnp.float32
    )
    self_delta = jnp.sum(self_probs * grad_self_probs, axis=-1)
    grad_self_scores = (
        self_probs * (grad_self_probs - self_delta[:, :, None]) * self_scale
    ).astype(jnp.bfloat16)
    grad_self_queries = (
        jnp.einsum("hqk,khd->qhd", grad_self_scores, keys_heads, preferred_element_type=jnp.float32)
        .reshape(LAT_DEV, D)
        .astype(jnp.bfloat16)
    )
    key_terms = jnp.einsum(
        "hqk,qhd->khd", grad_self_scores, self_queries, preferred_element_type=jnp.float32
    ).reshape(lat_count, D)
    value_terms = jnp.einsum(
        "hqk,qhd->khd", self_low, grad_heads, preferred_element_type=jnp.float32
    ).reshape(lat_count, D)
    key_share, value_share = (
        lax.psum_scatter(key_terms, "ctx", scatter_dimension=0, tiled=True),
        lax.psum_scatter(value_terms, "ctx", scatter_dimension=0, tiled=True),
    )
    key_low = key_share.astype(jnp.bfloat16)
    value_low = value_share.astype(jnp.bfloat16)
    grad_query_self = outer_sum(normed_two, grad_self_queries)
    grad_key_self = outer_sum(normed_two, key_low)
    grad_value_self = outer_sum(normed_two, value_low)
    grad_normed_two = (
        transposed(grad_self_queries, back_weights[6])
        + transposed(key_low, back_weights[7])
        + transposed(value_low, back_weights[8])
    )
    norm_out, norm_pull = jax.vjp(layer_norm, residual_two, gain_self)
    grad_res, grad_gain_self = norm_pull(grad_normed_two)
    grad_two = grad_three + grad_res
    grad_one, grad_up_cross, grad_down_cross, grad_gain_cross_mlp = mlp_back(
        grad_two,
        residual_one,
        gain_cross_mlp,
        normed_one,
        hidden_one,
        active_one,
        back_weights[4],
        back_weights[5],
    )
    grad_attn_low = grad_one.astype(jnp.bfloat16)
    grad_out_cross = outer_sum(attended, grad_attn_low)
    grad_attended = transposed(grad_attn_low, back_weights[3]).astype(jnp.bfloat16)
    back_queries, grad_att_all = (
        lax.all_gather(queries, "ctx", axis=0, tiled=True),
        lax.all_gather(grad_attended, "ctx", axis=0, tiled=True),
    )
    back_probs = recompute_probs(cross_scores(back_queries))
    back_low = back_probs.astype(jnp.bfloat16)
    grad_cross_probs = jnp.einsum(
        "qd,kd->qk", grad_att_all, values_cross, preferred_element_type=jnp.float32
    )
    delta_part = jnp.sum(back_probs * grad_cross_probs, axis=1)
    cross_delta = lax.psum(delta_part, "ctx")
    grad_cross_scores = (
        back_probs * (grad_cross_probs - cross_delta[:, None]) * cross_scale
    ).astype(jnp.bfloat16)
    key_grad = jnp.einsum(
        "qk,qd->kd", grad_cross_scores, back_queries, preferred_element_type=jnp.float32
    ).astype(jnp.bfloat16)
    value_grad = jnp.einsum(
        "qk,qd->kd", back_low, grad_att_all, preferred_element_type=jnp.float32
    ).astype(jnp.bfloat16)
    query_grad = lax.psum_scatter(
        matmul(grad_cross_scores, keys_cross), "ctx", scatter_dimension=0, tiled=True
    ).astype(jnp.bfloat16)
    grad_query_cross = outer_sum(normed_lat, query_grad)
    norm_out, norm_pull = jax.vjp(layer_norm, lat_in, gain_latent)
    grad_res, grad_gain_latent = norm_pull(transposed(query_grad, back_weights[0]))
    grad_latents = (grad_one + grad_res)[None]
    grad_key_cross = outer_sum(normed_pix, key_grad)
    grad_value_cross = outer_sum(normed_pix, value_grad)
    grad_normed_pix = transposed(key_grad, back_weights[1]) + transposed(
        value_grad, back_weights[2]
    )
    norm_out, norm_pull = jax.vjp(layer_norm, pix_in, gain_input)
    grad_pix, grad_gain_input = norm_pull(grad_normed_pix)
    shards_summed = (
        lax.psum_scatter(grad_query_cross, "fsdp", scatter_dimension=0, tiled=True),
        lax.psum_scatter(grad_key_cross, "fsdp", scatter_dimension=1, tiled=True),
        lax.psum_scatter(grad_value_cross, "fsdp", scatter_dimension=1, tiled=True),
        lax.psum_scatter(grad_out_cross, "fsdp", scatter_dimension=0, tiled=True),
        lax.psum_scatter(grad_up_cross, "fsdp", scatter_dimension=0, tiled=True),
        lax.psum_scatter(grad_down_cross, "fsdp", scatter_dimension=0, tiled=True),
        lax.psum_scatter(grad_query_self, "fsdp", scatter_dimension=0, tiled=True),
        lax.psum_scatter(grad_key_self, "fsdp", scatter_dimension=0, tiled=True),
        lax.psum_scatter(grad_value_self, "fsdp", scatter_dimension=0, tiled=True),
        lax.psum_scatter(grad_out_self, "fsdp", scatter_dimension=0, tiled=True),
        lax.psum_scatter(grad_up_self, "fsdp", scatter_dimension=0, tiled=True),
        lax.psum_scatter(grad_down_self, "fsdp", scatter_dimension=0, tiled=True),
    )
    totals = lax.psum(
        (
            shards_summed[0],
            shards_summed[1],
            shards_summed[2],
            shards_summed[3],
            shards_summed[4],
            shards_summed[5],
            shards_summed[6],
            shards_summed[7],
            shards_summed[8],
            shards_summed[9],
            shards_summed[10],
            shards_summed[11],
        ),
        "ctx",
    )
    gain_sums = lax.psum(
        (
            grad_gain_input,
            grad_gain_latent,
            grad_gain_cross_mlp,
            grad_gain_self,
            grad_gain_self_mlp,
        ),
        ("ctx", "fsdp"),
    )
    return (
        layer_out,
        grad_pix[None],
        grad_latents,
        totals[0],
        totals[1],
        totals[2],
        totals[3],
        totals[4],
        totals[5],
        totals[6],
        totals[7],
        totals[8],
        totals[9],
        totals[10],
        totals[11],
        gain_sums[0],
        gain_sums[1],
        gain_sums[2],
        gain_sums[3],
        gain_sums[4],
    )


def solution(mesh):
    placed = (
        P("fsdp", "ctx", None),
        P("fsdp", "ctx", None),
        P("fsdp", "ctx", None),
        P("fsdp", None),
        P("fsdp", None),
        P(),
        P("fsdp", None),
        P(None, "fsdp"),
        P(None, "fsdp"),
        P("fsdp", None),
        P("fsdp", None),
        P("fsdp", None),
        P("fsdp", None),
        P("fsdp", None),
        P("fsdp", None),
        P("fsdp", None),
        P("fsdp", None),
        P("fsdp", None),
        P(),
        P(),
        P(),
        P(),
        P(),
    )
    return jax.shard_map(
        local,
        mesh=mesh,
        in_specs=placed,
        out_specs=(
            P("fsdp", "ctx", None),
            P("fsdp", "ctx", None),
            P("fsdp", "ctx", None),
            P("fsdp", None),
            P(None, "fsdp"),
            P(None, "fsdp"),
            P("fsdp", None),
            P("fsdp", None),
            P("fsdp", None),
            P("fsdp", None),
            P("fsdp", None),
            P("fsdp", None),
            P("fsdp", None),
            P("fsdp", None),
            P("fsdp", None),
            P(),
            P(),
            P(),
            P(),
            P(),
        ),
        check_vma=False,
    )
```

profile of v0, /device:TPU:0, one launch (start us, length us, event | category | flops | bytes accessed | tf_op | source)
XLA Modules:
  0.0 1919.7 jit_solution(8346969673658302318)
XLA Ops:
  9.9 49.0 %all-gather.17.cloned.1.call-done = bf16[1024,1024]{1,0:T(8,128)(2,1)} async-done(((bf16[256,1024]{1,0:T(8,128)(2,1)}), bf16[1024,1024]{1,0:T(8,128)(2,1)}) %all-gather.17.cloned.1.call-update) | async-done | bytes 2097168 | tf_op jit(solution)/shard_map/all_gather | solution.py:120
  63.6 16.0 all_gather.80
  79.6 15.2 all_gather.75
  143.5 46.3 %reduce-scatter.17.cloned.1.call-done = f32[128,1024]{1,0:T(8,128)} async-done(((f32[1024,1024]{1,0:T(8,128)}), f32[128,1024]{1,0:T(8,128)}) %reduce-scatter.17.cloned.1.call-update) | async-done | bytes 524304 | tf_op jit(solution)/shard_map/reduce_scatter | solution.py:160
  192.4 45.5 %all-gather.23.cloned.1.call-done = bf16[1024,1024]{1,0:T(8,128)(2,1)} async-done(((bf16[256,1024]{1,0:T(8,128)(2,1)}), bf16[1024,1024]{1,0:T(8,128)(2,1)}) %all-gather.23.cloned.1.call-update) | async-done | bytes 2097168 | tf_op jit(solution)/shard_map/all_gather | solution.py:124
  240.0 44.6 %all-gather.25.cloned.1.call-done = bf16[1024,1024]{1,0:T(8,128)(2,1)} async-done(((bf16[256,1024]{1,0:T(8,128)(2,1)}), bf16[1024,1024]{1,0:T(8,128)(2,1)}) %all-gather.25.cloned.1.call-update) | async-done | bytes 2097168 | tf_op jit(solution)/shard_map/all_gather | solution.py:125
  287.3 44.3 %all-gather.33.cloned.1.call-done = bf16[1024,1024]{1,0:T(8,128)(2,1)} async-done(((bf16[256,1024]{1,0:T(8,128)(2,1)}), bf16[1024,1024]{1,0:T(8,128)(2,1)}) %all-gather.33.cloned.1.call-update) | async-done | bytes 2097168 | tf_op jit(solution)/shard_map/all_gather | solution.py:127
  334.4 44.1 %all-gather.27.cloned.1.call-done = bf16[1024,1024]{1,0:T(8,128)(2,1)} async-done(((bf16[256,1024]{1,0:T(8,128)(2,1)}), bf16[1024,1024]{1,0:T(8,128)(2,1)}) %all-gather.27.cloned.1.call-update) | async-done | bytes 2097168 | tf_op jit(solution)/shard_map/all_gather | solution.py:128
  388.3 37.1 %all-gather.31.cloned.1.call-done = bf16[1024,1024]{1,0:T(8,128)(2,1)} async-done(((bf16[256,1024]{1,0:T(8,128)(2,1)}), bf16[1024,1024]{1,0:T(8,128)(2,1)}) %all-gather.31.cloned.1.call-update) | async-done | bytes 2097168 | tf_op jit(solution)/shard_map/all_gather | solution.py:126
  427.6 26.9 %all-gather.35.cloned.1.call-done = bf16[1024,1024]{1,0:T(8,128)(2,1)} async-done(((bf16[128,1024]{1,0:T(8,128)(2,1)}), bf16[1024,1024]{1,0:T(8,128)(2,1)}) %all-gather.35.cloned.1.call-update) | async-done | bytes 2097168 | tf_op jit(solution)/shard_map/all_gather | solution.py:175
  463.8 21.3 %all-gather.29.cloned.1.call-done = bf16[1024,1024]{1,0:T(8,128)(2,1)} async-done(((bf16[128,1024]{1,0:T(8,128)(2,1)}), bf16[1024,1024]{1,0:T(8,128)(2,1)}) %all-gather.29.cloned.1.call-update) | async-done | bytes 2097168 | tf_op jit(solution)/shard_map/all_gather | solution.py:176
  489.0 44.1 %all-gather.37.cloned.1.call-done = bf16[1024,1024]{1,0:T(8,128)(2,1)} async-done(((bf16[256,1024]{1,0:T(8,128)(2,1)}), bf16[1024,1024]{1,0:T(8,128)(2,1)}) %all-gather.37.cloned.1.call-update) | async-done | bytes 2097168 | tf_op jit(solution)/shard_map/all_gather | solution.py:129
  535.5 44.5 %all-gather.39.cloned.1.call-done = bf16[1024,1024]{1,0:T(8,128)(2,1)} async-done(((bf16[256,1024]{1,0:T(8,128)(2,1)}), bf16[1024,1024]{1,0:T(8,128)(2,1)}) %all-gather.39.cloned.1.call-update) | async-done | bytes 2097168 | tf_op jit(solution)/shard_map/all_gather | solution.py:130
  582.1 44.7 %all-gather.41.cloned.1.call-done = bf16[1024,1024]{1,0:T(8,128)(2,1)} async-done(((bf16[256,1024]{1,0:T(8,128)(2,1)}), bf16[1024,1024]{1,0:T(8,128)(2,1)}) %all-gather.41.cloned.1.call-update) | async-done | bytes 2097168 | tf_op jit(solution)/shard_map/all_gather | solution.py:131
  639.3 13.6 fusion.8
  681.9 21.2 %reduce-scatter.19.cloned.1.call-done = f32[128,1024]{0,1:T(8,128)} async-done(((f32[1024,1024]{0,1:T(8,128)}), f32[128,1024]{0,1:T(8,128)}) %reduce-scatter.19.cloned.1.call-update) | async-done | bytes 524304 | tf_op jit(solution)/shard_map/reduce_scatter | solution.py:250
  705.8 51.9 %reduce-scatter.21.cloned.1.call-done = f32[128,1024]{0,1:T(8,128)} async-done(((f32[1024,1024]{0,1:T(8,128)}), f32[128,1024]{0,1:T(8,128)}) %reduce-scatter.21.cloned.1.call-update) | async-done | bytes 524304 | tf_op jit(solution)/shard_map/reduce_scatter | solution.py:251
  768.0 28.0 %all-gather.43.cloned.1.call-done = bf16[1024,1024]{1,0:T(8,128)(2,1)} async-done(((bf16[128,1024]{1,0:T(8,128)(2,1)}), bf16[1024,1024]{1,0:T(8,128)(2,1)}) %all-gather.43.cloned.1.call-update) | async-done | bytes 2097168 | tf_op jit(solution)/shard_map/all_gather | solution.py:281
  883.0 74.9 %reduce-scatter.45.cloned.1.call-done = f32[256,1024]{1,0:T(8,128)} async-done(((f32[1024,1024]{1,0:T(8,128)}), f32[256,1024]{1,0:T(8,128)}) %reduce-scatter.45.cloned.1.call-update) | async-done | bytes 1048592 | tf_op jit(solution)/shard_map/reduce_scatter | solution.py:324
  957.9 79.6 %reduce-scatter.37.cloned.1.call-done = f32[256,1024]{1,0:T(8,128)} async-done(((f32[1024,1024]{1,0:T(8,128)}), f32[256,1024]{1,0:T(8,128)}) %reduce-scatter.37.cloned.1.call-update) | async-done | bytes 1048592 | tf_op jit(solution)/shard_map/reduce_scatter | solution.py:320
  1037.4 79.6 %reduce-scatter.43.cloned.1.call-done = f32[256,1024]{1,0:T(8,128)} async-done(((f32[1024,1024]{1,0:T(8,128)}), f32[256,1024]{1,0:T(8,128)}) %reduce-scatter.43.cloned.1.call-update) | async-done | bytes 1048592 | tf_op jit(solution)/shard_map/reduce_scatter | solution.py:323
  1117.0 79.7 %reduce-scatter.47.cloned.1.call-done = f32[256,1024]{1,0:T(8,128)} async-done(((f32[1024,1024]{1,0:T(8,128)}), f32[256,1024]{1,0:T(8,128)}) %reduce-scatter.47.cloned.1.call-update) | async-done | bytes 1048592 | tf_op jit(solution)/shard_map/reduce_scatter | solution.py:325
  1196.7 30.5 %reduce-scatter.29.cloned.1.call-done = f32[261,256]{1,0:T(8,128)} async-done(((f32[261,1024]{1,0:T(8,128)}), f32[261,256]{1,0:T(8,128)}) %reduce-scatter.29.cloned.1.call-update) | async-done | bytes 267280 | tf_op jit(solution)/shard_map/reduce_scatter | solution.py:316
  1227.2 28.5 %reduce-scatter.27.cloned.1.call-done = f32[261,256]{1,0:T(8,128)} async-done(((f32[261,1024]{1,0:T(8,128)}), f32[261,256]{1,0:T(8,128)}) %reduce-scatter.27.cloned.1.call-update) | async-done | bytes 267280 | tf_op jit(solution)/shard_map/reduce_scatter | solution.py:315
  1255.8 77.7 %reduce-scatter.31.cloned.1.call-done = f32[256,1024]{1,0:T(8,128)} async-done(((f32[1024,1024]{1,0:T(8,128)}), f32[256,1024]{1,0:T(8,128)}) %reduce-scatter.31.cloned.1.call-update) | async-done | bytes 1048592 | tf_op jit(solution)/shard_map/reduce_scatter | solution.py:317
  1333.5 79.6 %reduce-scatter.35.cloned.1.call-done = f32[256,1024]{1,0:T(8,128)} async-done(((f32[1024,1024]{1,0:T(8,128)}), f32[256,1024]{1,0:T(8,128)}) %reduce-scatter.35.cloned.1.call-update) | async-done | bytes 1048592 | tf_op jit(solution)/shard_map/reduce_scatter | solution.py:319
  1413.1 79.4 %reduce-scatter.33.cloned.1.call-done = f32[256,1024]{1,0:T(8,128)} async-done(((f32[1024,1024]{1,0:T(8,128)}), f32[256,1024]{1,0:T(8,128)}) %reduce-scatter.33.cloned.1.call-update) | async-done | bytes 1048592 | tf_op jit(solution)/shard_map/reduce_scatter | solution.py:318
  1492.5 79.7 %reduce-scatter.41.cloned.1.call-done = f32[256,1024]{1,0:T(8,128)} async-done(((f32[1024,1024]{1,0:T(8,128)}), f32[256,1024]{1,0:T(8,128)}) %reduce-scatter.41.cloned.1.call-update) | async-done | bytes 1048592 | tf_op jit(solution)/shard_map/reduce_scatter | solution.py:322
  1572.2 79.6 %reduce-scatter.39.cloned.1.call-done = f32[256,1024]{1,0:T(8,128)} async-done(((f32[1024,1024]{1,0:T(8,128)}), f32[256,1024]{1,0:T(8,128)}) %reduce-scatter.39.cloned.1.call-update) | async-done | bytes 1048592 | tf_op jit(solution)/shard_map/reduce_scatter | solution.py:321
  1651.8 79.6 %reduce-scatter.25.cloned.1.call-done = f32[256,1024]{1,0:T(8,128)} async-done(((f32[1024,1024]{1,0:T(8,128)}), f32[256,1024]{1,0:T(8,128)}) %reduce-scatter.25.cloned.1.call-update) | async-done | bytes 1048592 | tf_op jit(solution)/shard_map/reduce_scatter | solution.py:314
  1742.1 42.6 %all-reduce = (f32[261]{0:T(512)}, f32[1024]{0:T(1024)}, f32[1024]{0:T(1024)}, f32[1024]{0:T(1024)}, f32[1024]{0:T(1024)}) all-reduce(f32[261]{0:T(512)S(1)} %get-tuple-element.215, f32[1024]{0:T(1024)S(1)} %get-tuple-element.223, f32[1024]{0:T(1024)S(1)} %get-tuple-element.221, ...), channel_id=1, replica_groups=mesh['ctx'=8,'fsdp'=4] {'ctx','fsdp'}, use_global_device_ids=true, to_apply=%region_61.62 | all-reduce | flops 4357 | bytes 34856 | tf_op jit(solution)/shard_map/psum | solution.py:344
  1785.7 114.1 %all-reduce.4.cloned.1.call-done = (f32[256,1024]{1,0:T(8,128)}, f32[261,256]{1,0:T(8,128)}, f32[261,256]{1,0:T(8,128)}, f32[256,1024]{1,0:T(8,128)}, f32[256,10...) async-done(((f32[256,1024]{1,0:T(8,128)}, ...) | async-done | bytes 11020304 | tf_op jit(solution)/shard_map/psum | solution.py:327
  (348 shorter events, 260.8 us)
Async XLA Ops:
  7.2 51.6 %all-gather.17.cloned.1.call-start = ((), (), s32[]{:S(2)}) async-start(), calls=%async_computation.16 | async-start | bytes 2621440 | tf_op jit(solution)/shard_map/all_gather | solution.py:120
  9.4 89.7 %all-gather.19.cloned.1.call-start = ((), (), s32[]{:S(2)}) async-start(), calls=%async_computation.17 | async-start | bytes 2359296 | tf_op jit(solution)/shard_map/all_gather | solution.py:140
  61.7 81.9 %all-gather.21.cloned.1.call-start = ((), (), s32[]{:S(2)}) async-start(), calls=%async_computation.19 | async-start | bytes 2621440 | tf_op jit(solution)/shard_map/all_gather | solution.py:123
  62.6 127.2 %reduce-scatter.17.cloned.1.call-start = ((), (), s32[]{:S(2)}) async-start(), calls=%async_computation.18 | async-start | bytes 4718592 | tf_op jit(solution)/shard_map/reduce_scatter | solution.py:160
  136.6 101.4 %all-gather.23.cloned.1.call-start = ((), (), s32[]{:S(2)}) async-start(), calls=%async_computation.20 | async-start | bytes 2621440 | tf_op jit(solution)/shard_map/all_gather | solution.py:124
  138.6 146.0 %all-gather.25.cloned.1.call-start = ((), (), s32[]{:S(2)}) async-start(), calls=%async_computation.21 | async-start | bytes 2621440 | tf_op jit(solution)/shard_map/all_gather | solution.py:125
  139.6 192.0 %all-gather.33.cloned.1.call-start = ((), (), s32[]{:S(2)}) async-start(), calls=%async_computation.25 | async-start | bytes 2621440 | tf_op jit(solution)/shard_map/all_gather | solution.py:127
  140.9 237.6 %all-gather.27.cloned.1.call-start = ((), (), s32[]{:S(2)}) async-start(), calls=%async_computation.22 | async-start | bytes 2621440 | tf_op jit(solution)/shard_map/all_gather | solution.py:128
  141.9 283.5 %all-gather.31.cloned.1.call-start = ((), (), s32[]{:S(2)}) async-start(), calls=%async_computation.24 | async-start | bytes 2621440 | tf_op jit(solution)/shard_map/all_gather | solution.py:126
  143.2 94.7 %copy-start.54 = (f32[1024]{0:T(1024)S(1)}, f32[1024]{0:T(1024)}, u32[]{:S(2)}) copy-start(f32[1024]{0:T(1024)} %param.45) | copy-start | bytes 12292
  143.2 311.3 %all-gather.35.cloned.1.call-start = ((), (), s32[]{:S(2)}) async-start(), calls=%async_computation.26 | async-start | bytes 2359296 | tf_op jit(solution)/shard_map/all_gather | solution.py:175
  334.3 150.7 %all-gather.29.cloned.1.call-start = ((), (), s32[]{:S(2)}) async-start(), calls=%async_computation.23 | async-start | bytes 2359296 | tf_op jit(solution)/shard_map/all_gather | solution.py:176
  381.2 151.9 %all-gather.37.cloned.1.call-start = ((), (), s32[]{:S(2)}) async-start(), calls=%async_computation.27 | async-start | bytes 2621440 | tf_op jit(solution)/shard_map/all_gather | solution.py:129
  383.4 196.6 %all-gather.39.cloned.1.call-start = ((), (), s32[]{:S(2)}) async-start(), calls=%async_computation.28 | async-start | bytes 2621440 | tf_op jit(solution)/shard_map/all_gather | solution.py:130
  385.6 241.2 %all-gather.41.cloned.1.call-start = ((), (), s32[]{:S(2)}) async-start(), calls=%async_computation.29 | async-start | bytes 2621440 | tf_op jit(solution)/shard_map/all_gather | solution.py:131
  387.8 315.3 %reduce-scatter.19.cloned.1.call-start = ((), (), s32[]{:S(2)}) async-start(), calls=%async_computation.30 | async-start | bytes 4718592 | tf_op jit(solution)/shard_map/reduce_scatter | solution.py:250
  652.8 104.8 %reduce-scatter.21.cloned.1.call-start = ((), (), s32[]{:S(2)}) async-start(), calls=%async_computation.31 | async-start | bytes 4718592 | tf_op jit(solution)/shard_map/reduce_scatter | solution.py:251
  657.9 138.1 %all-gather.43.cloned.1.call-start = ((), (), s32[]{:S(2)}) async-start(), calls=%async_computation.32 | async-start | bytes 2359296 | tf_op jit(solution)/shard_map/all_gather | solution.py:281
  767.9 110.9 %reduce-scatter.23.cloned.1.call-start = ((), (), s32[]{:S(2)}) async-start(), calls=%async_computation.33 | async-start | bytes 4718592 | tf_op jit(solution)/shard_map/reduce_scatter | solution.py:299
  827.3 130.5 %reduce-scatter.45.cloned.1.call-start = ((), (), s32[]{:S(2)}) async-start(), calls=%async_computation.44 | async-start | bytes 5242880 | tf_op jit(solution)/shard_map/reduce_scatter | solution.py:324
  831.4 206.1 %reduce-scatter.37.cloned.1.call-start = ((), (), s32[]{:S(2)}) async-start(), calls=%async_computation.40 | async-start | bytes 5242880 | tf_op jit(solution)/shard_map/reduce_scatter | solution.py:320
  835.1 282.0 %reduce-scatter.43.cloned.1.call-start = ((), (), s32[]{:S(2)}) async-start(), calls=%async_computation.43 | async-start | bytes 5242880 | tf_op jit(solution)/shard_map/reduce_scatter | solution.py:323
  838.8 357.9 %reduce-scatter.47.cloned.1.call-start = ((), (), s32[]{:S(2)}) async-start(), calls=%async_computation.45 | async-start | bytes 5242880 | tf_op jit(solution)/shard_map/reduce_scatter | solution.py:325
  842.7 384.5 %reduce-scatter.29.cloned.1.call-start = ((), (), s32[]{:S(2)}) async-start(), calls=%async_computation.36 | async-start | bytes 1351680 | tf_op jit(solution)/shard_map/reduce_scatter | solution.py:316
  851.2 404.5 %reduce-scatter.27.cloned.1.call-start = ((), (), s32[]{:S(2)}) async-start(), calls=%async_computation.35 | async-start | bytes 1351680 | tf_op jit(solution)/shard_map/reduce_scatter | solution.py:315
  859.0 474.5 %reduce-scatter.31.cloned.1.call-start = ((), (), s32[]{:S(2)}) async-start(), calls=%async_computation.37 | async-start | bytes 5242880 | tf_op jit(solution)/shard_map/reduce_scatter | solution.py:317
  862.8 550.3 %reduce-scatter.35.cloned.1.call-start = ((), (), s32[]{:S(2)}) async-start(), calls=%async_computation.39 | async-start | bytes 5242880 | tf_op jit(solution)/shard_map/reduce_scatter | solution.py:319
  866.7 625.9 %reduce-scatter.33.cloned.1.call-start = ((), (), s32[]{:S(2)}) async-start(), calls=%async_computation.38 | async-start | bytes 5242880 | tf_op jit(solution)/shard_map/reduce_scatter | solution.py:318
  870.4 701.8 %reduce-scatter.41.cloned.1.call-start = ((), (), s32[]{:S(2)}) async-start(), calls=%async_computation.42 | async-start | bytes 5242880 | tf_op jit(solution)/shard_map/reduce_scatter | solution.py:322
  874.2 777.6 %reduce-scatter.39.cloned.1.call-start = ((), (), s32[]{:S(2)}) async-start(), calls=%async_computation.41 | async-start | bytes 5242880 | tf_op jit(solution)/shard_map/reduce_scatter | solution.py:321
  878.0 853.4 %reduce-scatter.25.cloned.1.call-start = ((), (), s32[]{:S(2)}) async-start(), calls=%async_computation.34 | async-start | bytes 5242880 | tf_op jit(solution)/shard_map/reduce_scatter | solution.py:314
  882.7 1017.2 %all-reduce.4.cloned.1.call-start = ((), (), s32[]{:S(2)}) async-start(), calls=%async_computation.46 | async-start | bytes 22052864 | tf_op jit(solution)/shard_map/psum | solution.py:327
  (64 other events, 821.1 us)
Sparse Core Ops, SparseCore 0:
  10.2 48.6 all-gather.16
  61.8 26.6 all-gather.18
  90.6 45.9 all-gather.20
  139.8 50.0 reduce-scatter.16
  191.9 45.9 all-gather.22
  240.0 44.6 all-gather.24
  286.9 44.6 all-gather.32
  333.8 44.6 all-gather.26
  380.7 44.6 all-gather.30
  427.9 26.5 all-gather.34
  457.1 27.8 all-gather.28
  487.1 45.9 all-gather.36
  535.3 44.6 all-gather.38
  582.1 44.6 all-gather.40
  653.0 50.0 reduce-scatter.18
  706.3 51.2 reduce-scatter.20
  768.0 27.8 all-gather.42
  827.4 51.3 reduce-scatter.22
  881.1 76.7 reduce-scatter.44
  960.1 77.2 reduce-scatter.36
  1039.7 77.2 reduce-scatter.42
  1119.4 77.2 reduce-scatter.46
  1199.0 28.1 reduce-scatter.28
  1229.4 26.3 reduce-scatter.26
  1258.1 75.4 reduce-scatter.30
  1335.8 77.2 reduce-scatter.34
  1415.2 77.2 reduce-scatter.32
  1494.9 77.2 reduce-scatter.40
  1574.5 77.2 reduce-scatter.38
  1654.0 77.2 reduce-scatter.24
  1737.4 162.3 all-reduce.3
where the time goes:
time: 1930 us; the launch traced here: 1920 us
  waiting for transfers between devices  1560 us (81%)
  matrix products  163 us (8%)
  blocking collectives  105 us (5%)
  local copies, waits for them, and re-layouts  37.4 us (2%)
  other arithmetic  30.4 us (2%)
    psum x1, waiting for transfers between devices, local(): lax.psum((shards_summed[0], shards_summed[1], shards_summed[2], shards_su...  114 us
    reduce_scatter x1, waiting for transfers between devices, local(): lax.psum_scatter(grad_value_self, 'fsdp', scatter_dimension=0, tiled=True)  79.7 us
    reduce_scatter x1, waiting for transfers between devices, local(): lax.psum_scatter(grad_down_self, 'fsdp', scatter_dimension=0, tiled=True)  79.7 us
    reduce_scatter x1, waiting for transfers between devices, local(): lax.psum_scatter(grad_out_self, 'fsdp', scatter_dimension=0, tiled=True)  79.6 us
    reduce_scatter x1, waiting for transfers between devices, local(): lax.psum_scatter(grad_down_cross, 'fsdp', scatter_dimension=0, tiled=True)  79.6 us
    reduce_scatter x1, waiting for transfers between devices, local(): lax.psum_scatter(grad_key_self, 'fsdp', scatter_dimension=0, tiled=True)  79.6 us
    reduce_scatter x1, waiting for transfers between devices, local(): lax.psum_scatter(grad_query_self, 'fsdp', scatter_dimension=0, tiled=True)  79.6 us
    reduce_scatter x1, waiting for transfers between devices, local(): lax.psum_scatter(grad_query_cross, 'fsdp', scatter_dimension=0, tiled=True)  79.6 us
  transfers between devices with their start and end apart: 31, of which 29 were waited for; matrix products, arithmetic and copies ran while one was open for 8% of the time, Pallas kernels for 0%

commit v1 on v0

v1 whole, which is shorter than its diff:
```python
import math

import jax
import jax.numpy as jnp
from jax import lax
from jax.sharding import PartitionSpec as P

D = 1024
HEADS = 8
HEAD = D // HEADS
STRIDE = 8
LBLK = 64
BF = jnp.bfloat16
F32 = jnp.float32
CROSS_SCALE = 1.0 / math.sqrt(D)
SELF_SCALE = 1.0 / math.sqrt(HEAD)
MASKED = -1e30
GELU_K = math.sqrt(2.0 / math.pi)
GELU_A = 0.044715


def mm(a, b):
    return jnp.dot(a, b, preferred_element_type=F32)


def mm_nt(a, b):
    return lax.dot_general(a, b, (((1,), (1,)), ((), ())), preferred_element_type=F32)


def mm_tn(a, b):
    return lax.dot_general(a, b, (((0,), (0,)), ((), ())), preferred_element_type=F32)


def norm_parts(x):
    center = x - jnp.mean(x, axis=-1, keepdims=True)
    r = lax.rsqrt(jnp.mean(center * center, axis=-1, keepdims=True) + 1e-05)
    return center * r, r


def norm_back(dy, x, gain):
    hat, r = norm_parts(x)
    dhat = dy * gain
    dx = r * (
        dhat
        - jnp.mean(dhat, axis=-1, keepdims=True)
        - hat * jnp.mean(dhat * hat, axis=-1, keepdims=True)
    )
    return dx, jnp.sum(dy * hat, axis=0)


def gelu(u):
    return 0.5 * u * (1.0 + jnp.tanh(GELU_K * (u + GELU_A * u * u * u)))


def gelu_slope(u):
    t = jnp.tanh(GELU_K * (u + GELU_A * u * u * u))
    return 0.5 * (1.0 + t) + 0.5 * u * (1.0 - t * t) * GELU_K * (1.0 + 3.0 * GELU_A * u * u)


def intervals(lengths, offsets, deal):
    count = lengths.shape[0]
    before = jnp.arange(count)[:, None] > jnp.arange(count)[None, :]
    starts = jnp.sum(jnp.where(before, lengths[None, :], 0), axis=1)
    base = (deal[:, None] * LBLK + jnp.arange(LBLK, dtype=jnp.int32)[None, :]).reshape(-1)
    pos = base * STRIDE + offsets
    lo = jnp.max(jnp.where(starts[None, :] <= pos[:, None], starts[None, :], -1), axis=1)
    return lo, pos


def plain(
    pixels, latents, cotangent, doc_lengths, latent_offsets, block_deal,
    wq_c, wk_c, wv_c, wo_c, wu_c, wd_c, wq_s, wk_s, wv_s, wo_s, wu_s, wd_s,
    g_in, g_lat, g_cmlp, g_self, g_smlp,
):
    n = lax.axis_size("ctx")
    me = lax.axis_index("ctx")
    rows = latents.shape[1]
    npix = pixels.shape[1]
    c = pixels.shape[2]
    lo, pos = intervals(doc_lengths[0], latent_offsets[0], block_deal)
    own_lo = lax.dynamic_slice_in_dim(lo, me * rows, rows)
    own_pos = lax.dynamic_slice_in_dim(pos, me * rows, rows)
    pix_pos = me * npix + jnp.arange(npix, dtype=jnp.int32)
    mask = (lo[:, None] <= pix_pos[None, :]) & (pix_pos[None, :] <= pos[:, None])
    smask = (own_lo[:, None] <= pos[None, :]) & (pos[None, :] <= own_pos[:, None])

    wq_c, wk_c, wv_c, wo_c = (w.astype(BF) for w in (wq_c, wk_c, wv_c, wo_c))
    wk_all = lax.all_gather(wk_c, "fsdp", axis=1, tiled=True)
    wqk = lax.all_gather(mm_nt(wq_c, wk_all).astype(BF), "fsdp", axis=0, tiled=True)
    wvo = lax.psum(mm(wv_c, wo_c), "fsdp").astype(BF)
    big = jnp.stack([w.astype(BF) for w in (wu_c, wd_c, wq_s, wk_s, wv_s, wo_s, wu_s, wd_s)])
    wu1, wd1, wq, wk, wv, wo, wu3, wd3 = lax.all_gather(big, "fsdp", axis=1, tiled=True)

    xin = pixels[0].astype(F32)
    xn = (norm_parts(xin)[0] * g_in).astype(BF)
    lat = latents[0].astype(F32)
    ln = (norm_parts(lat)[0] * g_lat).astype(BF)
    qk_all = lax.all_gather(mm(ln, wqk).astype(BF), "ctx", axis=0, tiled=True)
    s = jnp.where(mask, mm_nt(qk_all, xn) * CROSS_SCALE, MASKED)
    top = jnp.max(s, axis=1, keepdims=True)
    e = jnp.where(mask, jnp.exp(s - top), 0.0)
    total = jnp.sum(e, axis=1, keepdims=True)
    part = jnp.concatenate([mm(e.astype(BF), xn), top, total], axis=1)
    parts = lax.all_to_all(part.reshape(n, rows, c + 2), "ctx", 0, 0)
    tops = parts[:, :, c : c + 1]
    high = jnp.max(tops, axis=0)
    share = jnp.exp(tops - high[None])
    full = jnp.sum(share * parts[:, :, c + 1 :], axis=0)
    px = jnp.sum(share * parts[:, :, :c], axis=0) / full
    lse = high + jnp.log(full)
    px_low = px.astype(BF)
    h1 = lat + mm(px_low, wvo)
    n1 = (norm_parts(h1)[0] * g_cmlp).astype(BF)
    u1 = mm(n1, wu1)
    z1 = gelu(u1).astype(BF)
    h2 = h1 + mm(z1, wd1)
    n2 = (norm_parts(h2)[0] * g_self).astype(BF)
    q = mm(n2, wq).astype(BF).reshape(rows, HEADS, HEAD)
    kv = jnp.concatenate([mm(n2, wk), mm(n2, wv)], axis=1).astype(BF)
    kv = lax.all_gather(kv, "ctx", axis=0, tiled=True)
    k = kv[:, :D].reshape(n * rows, HEADS, HEAD)
    v = kv[:, D:].reshape(n * rows, HEADS, HEAD)
    ss = jnp.einsum("qhd,khd->hqk", q, k, preferred_element_type=F32) * SELF_SCALE
    ss = jnp.where(smask[None], ss, MASKED)
    se = jnp.exp(ss - jnp.max(ss, axis=-1, keepdims=True))
    ps = se / jnp.sum(se, axis=-1, keepdims=True)
    psl = ps.astype(BF)
    sa = jnp.einsum("hqk,khd->qhd", psl, v, preferred_element_type=F32)
    sa = sa.reshape(rows, D).astype(BF)
    h3 = h2 + mm(sa, wo)
    n3 = (norm_parts(h3)[0] * g_smlp).astype(BF)
    u3 = mm(n3, wu3)
    z3 = gelu(u3).astype(BF)
    layer_out = (h3 + mm(z3, wd3)).astype(BF)

    gy3 = cotangent[0]
    gu3 = (mm_nt(gy3, wd3) * gelu_slope(u3)).astype(BF)
    dx, gg_smlp = norm_back(mm_nt(gu3, wu3), h3, g_smlp)
    dh3 = gy3.astype(F32) + dx
    go3 = dh3.astype(BF)
    gas = mm_nt(go3, wo).astype(BF).reshape(rows, HEADS, HEAD)
    dps = jnp.einsum("qhd,khd->hqk", gas, v, preferred_element_type=F32)
    sdelta = jnp.sum(ps * dps, axis=-1, keepdims=True)
    dss = (ps * (dps - sdelta) * SELF_SCALE).astype(BF)
    dqs = jnp.einsum("hqk,khd->qhd", dss, k, preferred_element_type=F32)
    dqs = dqs.reshape(rows, D).astype(BF)
    dks = jnp.einsum("hqk,qhd->khd", dss, q, preferred_element_type=F32).reshape(n * rows, D)
    dvs = jnp.einsum("hqk,qhd->khd", psl, gas, preferred_element_type=F32).reshape(n * rows, D)
    dkv = lax.psum_scatter(
        jnp.concatenate([dks, dvs], axis=1), "ctx", scatter_dimension=0, tiled=True
    ).astype(BF)
    dks, dvs = dkv[:, :D], dkv[:, D:]
    dn2 = mm_nt(dqs, wq) + mm_nt(dks, wk) + mm_nt(dvs, wv)
    dx, gg_self = norm_back(dn2, h2, g_self)
    dh2 = dh3 + dx
    gy1 = dh2.astype(BF)
    gu1 = (mm_nt(gy1, wd1) * gelu_slope(u1)).astype(BF)
    dx, gg_cmlp = norm_back(mm_nt(gu1, wu1), h1, g_cmlp)
    dh1 = dh2 + dx
    go1 = dh1.astype(BF)
    gv = mm_nt(go1, wvo).astype(BF)
    delta = jnp.sum(px * gv.astype(F32), axis=1, keepdims=True)
    gv_all = lax.all_gather(gv, "ctx", axis=0, tiled=True)
    stat = lax.all_gather(jnp.concatenate([lse, delta], axis=1), "ctx", axis=0, tiled=True)
    p = jnp.where(mask, jnp.exp(s - stat[:, :1]), 0.0)
    ds = (p * (mm_nt(gv_all, xn) - stat[:, 1:]) * CROSS_SCALE).astype(BF)
    dxn = mm_tn(ds, qk_all) + mm_tn(p.astype(BF), gv_all)
    dpix, gg_in = norm_back(dxn, xin, g_in)
    dqk = lax.psum_scatter(mm(ds, xn), "ctx", scatter_dimension=0, tiled=True).astype(BF)
    dx, gg_lat = norm_back(mm_nt(dqk, wqk), lat, g_lat)
    dlat = dh1 + dx

    e_sum = lax.psum_scatter(mm_tn(ln, dqk), "fsdp", scatter_dimension=0, tiled=True)
    e_sum, f_sum = lax.psum((e_sum, lax.psum(mm_tn(px_low, go1), "fsdp")), "ctx")
    e_sum, f_sum = e_sum.astype(BF), f_sum.astype(BF)
    d_wq_c = mm(e_sum, wk_all)
    d_wk_c = lax.psum_scatter(mm_tn(e_sum, wq_c), "fsdp", scatter_dimension=1, tiled=True)
    d_wv_c = mm_nt(f_sum, wo_c)
    d_wo_c = mm_tn(wv_c, f_sum)
    pairs = ((n1, gu1), (z1, gy1), (n2, dqs), (n2, dks), (n2, dvs), (sa, go3), (n3, gu3), (z3, gy3))
    d_big = [
        lax.psum(lax.psum_scatter(mm_tn(a, b), "fsdp", scatter_dimension=0, tiled=True), "ctx")
        for a, b in pairs
    ]
    gains = lax.psum(jnp.concatenate([gg_in, gg_lat, gg_cmlp, gg_self, gg_smlp]), ("ctx", "fsdp"))
    return (
        layer_out[None], dpix[None], dlat[None], d_wq_c, d_wk_c, d_wv_c, d_wo_c, *d_big,
        gains[:c], gains[c : c + D], gains[c + D : c + 2 * D],
        gains[c + 2 * D : c + 3 * D], gains[c + 3 * D :],
    )


def solution(mesh):
    rows, row, col, all_ = P("fsdp", "ctx", None), P("fsdp", None), P(None, "fsdp"), P()
    weights = (row, col, col, *(row,) * 9)
    return jax.shard_map(
        plain,
        mesh=mesh,
        in_specs=(rows, rows, rows, row, row, all_, *weights, *(all_,) * 5),
        out_specs=(rows, rows, rows, *weights, *(all_,) * 5),
        check_vma=False,
    )
```

time: 1930 us -> 1520 us (0.79)
  waiting for transfers between devices: 1560 us -> 1020 us
  blocking collectives: 105 us -> 262 us
  matrix products: 163 us -> 137 us
    all_gather x14 -> x2, waiting for transfers between devices: 474 us -> 203 us  [the longest x1 170 us: plain(): lax.all_gather(big, 'fsdp', axis=1, tiled=True)]
    reduce_scatter x16 -> x12, waiting for transfers between devices: 968 us -> 698 us  [the longest x8 578 us: plain(): lax.psum_scatter(mm_tn(a, b), 'fsdp', scatter_dimension=0, tiled=True)]
    psum x2 -> x3, blocking collectives: 55.7 us -> 183 us  [the longest x1 86.6 us: plain(): wvo = lax.psum(mm(wv_c, wo_c), 'fsdp').astype(BF)]
    all_gather x4 -> x5, blocking collectives: 49.4 us -> 78.5 us  [the longest x1 32 us: plain(): lax.all_gather(mm_nt(wq_c, wk_all).astype(BF), 'fsdp', axis=0, tiled=True)]
    dot_general x47, matrix products: 158 us -> 131 us  [the longest x14 40.7 us: mm_tn(): lax.dot_general(a, b, (((0,), (0,)), ((), ())), preferred_element_type=F32)]
    psum x1 -> x2, waiting for transfers between devices: 114 us -> 121 us  [the longest x1 99.9 us: plain(): lax.psum(lax.psum_scatter(mm_tn(a, b), 'fsdp', scatter_dimension=0, tiled...]
  transfers between devices with their start and end apart: 31 -> 17, of which waited for: 29 -> 15; matrix products, arithmetic and copies ran while one was open for 8% -> 5% of each run, Pallas kernels for 0% -> 0%
where the time goes in v1:
time: 1520 us; the launch traced here: 1510 us
  waiting for transfers between devices  1020 us (67%)
  blocking collectives  262 us (17%)
  matrix products  137 us (9%)
  local copies, waits for them, and re-layouts  37.8 us (2%)
  other arithmetic  28.7 us (2%)
  between operations  15.6 us (1%)
    reduce_scatter x8, waiting for transfers between devices, plain(): lax.psum_scatter(mm_tn(a, b), 'fsdp', scatter_dimension=0, tiled=True)  578 us
    all_gather x1, waiting for transfers between devices, plain(): lax.all_gather(big, 'fsdp', axis=1, tiled=True)  170 us
    psum x1, waiting for transfers between devices, plain(): lax.psum(lax.psum_scatter(mm_tn(a, b), 'fsdp', scatter_dimension=0, tiled...  99.9 us
    psum x1, blocking collectives, plain(): wvo = lax.psum(mm(wv_c, wo_c), 'fsdp').astype(BF)  86.6 us
    reduce_scatter x1, waiting for transfers between devices, plain(): lax.psum_scatter(jnp.concatenate([dks, dvs], axis=1), 'ctx', scatter_dime...  56.9 us
    psum x1, blocking collectives, plain(): lax.psum((e_sum, lax.psum(mm_tn(px_low, go1), 'fsdp')), 'ctx')  55.3 us
    psum x1, blocking collectives, plain(): lax.psum(jnp.concatenate([gg_in, gg_lat, gg_cmlp, gg_self, gg_smlp]), ('c...  41.5 us
    dot_general x14, matrix products, mm_tn(): lax.dot_general(a, b, (((0,), (0,)), ((), ())), preferred_element_type=F32)  40.7 us
  transfers between devices with their start and end apart: 17, of which 15 were waited for; matrix products, arithmetic and copies ran while one was open for 5% of the time, Pallas kernels for 0%

profile of v1, /device:TPU:0, one launch (start us, length us, event | category | flops | bytes accessed | tf_op | source)
XLA Modules:
  0.0 1508.5 jit_solution(5483614814375851525)
XLA Ops:
  19.2 18.6 %all_gather.21 = bf16[261,1024]{1,0:T(8,128)(2,1)S(1)} all-gather(bf16[261,256]{1,0:T(8,128)(2,1)S(1)} %convert_element_type.174), channel_id=1, replica_groups=mesh['ctx'=8,'fsdp'=4] {'fsdp'}, dimensions={1}, use_global_device_ids=true | all-gather | bytes 668160 | tf_op jit(solution)/shard_map/all_gather | solution.py:88
  39.0 32.0 %all_gather.22 = bf16[1024,261]{0,1:T(8,128)(2,1)S(1)} all-gather(bf16[256,261]{0,1:T(8,128)(2,1)S(1)} %convolution_convert_fusion), channel_id=1, replica_groups=mesh['ctx'=8,'fsdp'=4] {'fsdp'}, dimensions={0}, use_global_device_ids=true | all-gather | bytes 668160 | tf_op jit(solution)/shard_map/all_gather | solution.py:89
  71.4 10.0 all_gather.23
  93.1 86.6 %all-reduce.10 = bf16[261,1024]{1,0:T(8,128)(2,1)S(1)} all-reduce(f32[261,1024]{1,0:T(8,128)S(1)} %fusion.128), channel_id=1, replica_groups=mesh['ctx'=8,'fsdp'=4] {'fsdp'}, use_global_device_ids=true, to_apply=%region_11.12 | all-reduce | flops 267264 | bytes 1603584 | tf_op jit(solution)/shard_map/psum | solution.py:90
  181.2 170.2 %all-gather.3.cloned.1.call-done = bf16[8,1024,1024]{2,1,0:T(8,128)(2,1)} async-done(((bf16[8,256,1024]{2,1,0:T(8,128)(2,1)}), bf16[8,1024,1024]{2,1,0:T(8,128)(2,1)}) %all-gather.3.cloned.1.call-update) | async-done | bytes 16777232 | tf_op jit(solution)/shard_map/all_gather | solution.py:92
  364.8 32.5 %all-gather.5.cloned.1.call-done = bf16[1024,2048]{1,0:T(8,128)(2,1)} async-done(((bf16[128,2048]{1,0:T(8,128)(2,1)}), bf16[1024,2048]{1,0:T(8,128)(2,1)}) %all-gather.5.cloned.1.call-update) | async-done | bytes 4194320 | tf_op jit(solution)/shard_map/all_gather | solution.py:120
  397.4 4.4 fusion.181
  401.8 4.1 copy.67
  405.9 6.0 fusion.186
  431.9 3.9 fusion.18
  438.6 13.6 fusion.8
  452.2 8.4 pad_maximum_fusion
  462.2 12.9 fusion.56
  475.2 56.9 %reduce-scatter.13.cloned.1.call-done = f32[128,2048]{0,1:T(8,128)} async-done(((f32[1024,2048]{0,1:T(8,128)}), f32[128,2048]{0,1:T(8,128)}) %reduce-scatter.13.cloned.1.call-update) | async-done | bytes 1048592 | tf_op jit(solution)/shard_map/reduce_scatter | solution.py:149
  547.5 8.8 all_gather.26
  556.3 9.1 all_gather.27
  574.0 33.8 %reduce-scatter.15.cloned.1.call-done = f32[128,261]{0,1:T(8,128)} async-done(((f32[1024,261]{0,1:T(8,128)}), f32[128,261]{0,1:T(8,128)}) %reduce-scatter.15.cloned.1.call-update) | async-done | bytes 133648 | tf_op jit(solution)/shard_map/reduce_scatter | solution.py:169
  622.2 3.9 fusion.124
  637.3 3.9 fusion.174
  641.3 21.6 %all-reduce.7.cloned.1.call-done = f32[261,1024]{1,0:T(8,128)} async-done(((f32[261,1024]{1,0:T(8,128)}), f32[261,1024]{1,0:T(8,128)}) %all-reduce.7.cloned.1.call-update) | async-done | bytes 1069072 | tf_op jit(solution)/shard_map/psum | solution.py:174
  662.9 29.3 %reduce-scatter.17.cloned.1.call-done = f32[256,261]{0,1:T(8,128)} async-done(((f32[1024,261]{0,1:T(8,128)}), f32[256,261]{0,1:T(8,128)}) %reduce-scatter.17.cloned.1.call-update) | async-done | bytes 267280 | tf_op jit(solution)/shard_map/reduce_scatter | solution.py:173
  692.1 55.3 %all-reduce.11 = (bf16[256,261]{0,1:T(8,128)(2,1)S(1)}, bf16[261,1024]{1,0:T(8,128)(2,1)}) all-reduce(f32[256,261]{0,1:T(8,128)} %reduce-scatter.17.cloned.1.call-done, f32[261,1024]{1,0:T(8,128)} %all-reduce.7.cloned.1.call-done), channel_id=1, replica_groups=mesh['ctx'=8,'fsdp'=4] {'ctx'}, use_global_device_ids=true, to_apply=%region_35.36 | all-reduce | flops 334080 | bytes 2004480 | tf_op jit(solution)/shard_map/psum | solution.py:174
  748.9 21.0 %reduce-scatter.33.cloned.1.call-done = f32[256,1024]{1,0:T(8,128)} async-done(((f32[1024,1024]{1,0:T(8,128)}), f32[256,1024]{1,0:T(8,128)}) %reduce-scatter.33.cloned.1.call-update) | async-done | bytes 1048592 | tf_op jit(solution)/shard_map/reduce_scatter | solution.py:182
  769.9 79.7 %reduce-scatter.31.cloned.1.call-done = f32[256,1024]{1,0:T(8,128)} async-done(((f32[1024,1024]{1,0:T(8,128)}), f32[256,1024]{1,0:T(8,128)}) %reduce-scatter.31.cloned.1.call-update) | async-done | bytes 1048592 | tf_op jit(solution)/shard_map/reduce_scatter | solution.py:182
  849.6 79.6 %reduce-scatter.25.cloned.1.call-done = f32[256,1024]{1,0:T(8,128)} async-done(((f32[1024,1024]{1,0:T(8,128)}), f32[256,1024]{1,0:T(8,128)}) %reduce-scatter.25.cloned.1.call-update) | async-done | bytes 1048592 | tf_op jit(solution)/shard_map/reduce_scatter | solution.py:182
  929.2 79.6 %reduce-scatter.35.cloned.1.call-done = f32[256,1024]{1,0:T(8,128)} async-done(((f32[1024,1024]{1,0:T(8,128)}), f32[256,1024]{1,0:T(8,128)}) %reduce-scatter.35.cloned.1.call-update) | async-done | bytes 1048592 | tf_op jit(solution)/shard_map/reduce_scatter | solution.py:182
  1008.7 79.6 %reduce-scatter.29.cloned.1.call-done = f32[256,1024]{1,0:T(8,128)} async-done(((f32[1024,1024]{1,0:T(8,128)}), f32[256,1024]{1,0:T(8,128)}) %reduce-scatter.29.cloned.1.call-update) | async-done | bytes 1048592 | tf_op jit(solution)/shard_map/reduce_scatter | solution.py:182
  1088.3 79.6 %reduce-scatter.27.cloned.1.call-done = f32[256,1024]{1,0:T(8,128)} async-done(((f32[1024,1024]{1,0:T(8,128)}), f32[256,1024]{1,0:T(8,128)}) %reduce-scatter.27.cloned.1.call-update) | async-done | bytes 1048592 | tf_op jit(solution)/shard_map/reduce_scatter | solution.py:182
  1167.9 79.6 %reduce-scatter.23.cloned.1.call-done = f32[256,1024]{1,0:T(8,128)} async-done(((f32[1024,1024]{1,0:T(8,128)}), f32[256,1024]{1,0:T(8,128)}) %reduce-scatter.23.cloned.1.call-update) | async-done | bytes 1048592 | tf_op jit(solution)/shard_map/reduce_scatter | solution.py:182
  1247.5 79.6 %reduce-scatter.21.cloned.1.call-done = f32[256,1024]{1,0:T(8,128)} async-done(((f32[1024,1024]{1,0:T(8,128)}), f32[256,1024]{1,0:T(8,128)}) %reduce-scatter.21.cloned.1.call-update) | async-done | bytes 1048592 | tf_op jit(solution)/shard_map/reduce_scatter | solution.py:182
  1338.7 41.5 %psum.103 = f32[4357]{0:T(1024)S(1)} all-reduce(f32[4357]{0:T(1024)S(1)} %concatenate.27), channel_id=1, replica_groups=mesh['ctx'=8,'fsdp'=4] {'ctx','fsdp'}, use_global_device_ids=true, to_apply=%region_60.61 | all-reduce | flops 4357 | bytes 34856 | tf_op jit(solution)/shard_map/psum | solution.py:185
  1391.0 99.9 %all-reduce.9.cloned.1.call-done = (f32[256,1024]{1,0:T(8,128)}, f32[256,1024]{1,0:T(8,128)}, f32[256,1024]{1,0:T(8,128)}, f32[256,1024]{1,0:T(8,128)}, f32[256,...) async-done(((f32[256,1024]{1,0:T(8,128)}, f32[256,1024]{1,0:T(8,128)}, f32[256,1024]{1,0:T(8,128)}, f32[256,1024]{1,0:T(8,128)}, ...) | async-done | bytes 8388624 | tf_op jit(solution)/shard_map/psum | solution.py:182
  (343 shorter events, 147.6 us)
Async XLA Ops:
  7.2 344.2 %all-gather.3.cloned.1.call-start = ((), (), s32[]{:S(2)}) async-start(), calls=%async_computation.13 | async-start | bytes 20971520 | tf_op jit(solution)/shard_map/all_gather | solution.py:92
  18.3 63.1 %copy-start.5 = (bf16[1,1024,261]{1,2,0:T(8,128)(2,1)S(1)}, bf16[1,1024,261]{1,2,0:T(8,128)(2,1)}, u32[]{:S(2)}) copy-start(bf16[1,1024,261]{1,2,0:T(8,128)(2,1)} %param.23) | copy-start | bytes 1603588
  18.3 63.4 %copy-start.82 = (f32[261]{0:T(512)S(1)}, f32[261]{0:T(512)}, u32[]{:S(2)}) copy-start(f32[261]{0:T(512)} %param.41) | copy-start | bytes 3136
  18.6 65.3 %copy-start.66 = (s32[1024]{0:T(1024)}, s32[1024]{0:T(1024)S(1)}, u32[]{:S(2)}) copy-start(s32[1024]{0:T(1024)S(1)} %iota_add_fusion) | copy-start | bytes 12292
  18.8 342.7 %copy-start.68 = (s32[1024]{0:T(1024)}, s32[1024]{0:T(1024)S(1)}, u32[]{:S(2)}) copy-start(s32[1024]{0:T(1024)S(1)} %select_reduce_fusion) | copy-start | bytes 12292
  87.8 263.6 %copy-start.61 = (f32[1024]{0:T(1024)S(1)}, f32[1024]{0:T(1024)}, u32[]{:S(2)}) copy-start(f32[1024]{0:T(1024)} %param.43) | copy-start | bytes 12292
  87.8 91.9 %all-to-all-start = ((f32[8,128,263]{1,2,0:T(8,128)}), f32[8,128,263]{1,2,0:T(8,128)S(1)}, u32[]{:S(2)}, u32[]{:S(2)}) async-start(f32[8,128,263]{1,2,0:T(8,128)} %pad_maximum_fusion.1), calls=%async_computation | async-start | bytes 2162688 | tf_op jit(solution)/shard_map/all_to_all | solution.py:104
  91.5 305.8 %all-gather.5.cloned.1.call-start = ((), (), s32[]{:S(2)}) async-start(), calls=%async_computation.14 | async-start | bytes 4718592 | tf_op jit(solution)/shard_map/all_gather | solution.py:120
  179.7 171.8 %copy-start.3 = (bf16[261,1024]{1,0:T(8,128)(2,1)}, bf16[261,1024]{1,0:T(8,128)(2,1)S(1)}, u32[]{:S(2)}) copy-start(bf16[261,1024]{1,0:T(8,128)(2,1)S(1)} %all-reduce.10) | copy-start | bytes 1603588
  179.8 176.2 %copy-start.70 = (f32[128]{0:T(128)}, f32[128]{0:T(128)S(1)}, u32[]{:S(2)}) copy-start(f32[128]{0:T(128)S(1)} %get-tuple-element.85) | copy-start | bytes 1540
  181.0 175.2 %copy-start.80 = (f32[128]{0:T(128)}, f32[128]{0:T(128)S(1)}, u32[]{:S(2)}) copy-start(f32[128]{0:T(128)S(1)} %broadcast_multiply_fusion.13) | copy-start | bytes 1540
  181.2 175.0 %copy-start.59 = (f32[1024]{0:T(1024)S(1)}, f32[1024]{0:T(1024)}, u32[]{:S(2)}) copy-start(f32[1024]{0:T(1024)} %param.44) | copy-start | bytes 12292
  181.2 175.2 %copy-start.84 = (f32[128]{0:T(128)}, f32[128]{0:T(128)S(1)}, u32[]{:S(2)}) copy-start(f32[128]{0:T(128)S(1)} %add_rsqrt_fusion.3) | copy-start | bytes 1540
  361.5 170.6 %reduce-scatter.13.cloned.1.call-start = ((), (), s32[]{:S(2)}) async-start(), calls=%async_computation.15 | async-start | bytes 9437184 | tf_op jit(solution)/shard_map/reduce_scatter | solution.py:149
  460.6 147.2 %reduce-scatter.15.cloned.1.call-start = ((), (), s32[]{:S(2)}) async-start(), calls=%async_computation.16 | async-start | bytes 1216512 | tf_op jit(solution)/shard_map/reduce_scatter | solution.py:169
  475.1 63.3 %copy-start.27 = (bf16[8,128,128]{2,1,0:T(8,128)(2,1)S(1)}, bf16[8,128,128]{2,1,0:T(8,128)(2,1)}, u32[]{:S(2)}) copy-start(bf16[8,128,128]{2,1,0:T(8,128)(2,1)} %fusion.56) | copy-start | bytes 786436
  475.2 63.3 %copy-start.75 = (f32[128]{0:T(128)S(1)}, f32[128]{0:T(128)}, u32[]{:S(2)}) copy-start(f32[128]{0:T(128)} %copy-done.74) | copy-start | bytes 1540
  475.2 63.4 %copy-start.79 = (f32[128]{0:T(128)S(1)}, f32[128]{0:T(128)}, u32[]{:S(2)}) copy-start(f32[128]{0:T(128)} %copy-done.78) | copy-start | bytes 1540
  571.6 91.2 %all-reduce.7.cloned.1.call-start = ((), (), s32[]{:S(2)}) async-start(), calls=%async_computation.19 | async-start | bytes 2162688 | tf_op jit(solution)/shard_map/psum | solution.py:174
  573.9 118.2 %reduce-scatter.17.cloned.1.call-start = ((), (), s32[]{:S(2)}) async-start(), calls=%async_computation.17 | async-start | bytes 1351680 | tf_op jit(solution)/shard_map/reduce_scatter | solution.py:173
  610.1 159.8 %reduce-scatter.33.cloned.1.call-start = ((), (), s32[]{:S(2)}) async-start(), calls=%async_computation.26 | async-start | bytes 5242880 | tf_op jit(solution)/shard_map/reduce_scatter | solution.py:182
  613.9 235.7 %reduce-scatter.31.cloned.1.call-start = ((), (), s32[]{:S(2)}) async-start(), calls=%async_computation.25 | async-start | bytes 5242880 | tf_op jit(solution)/shard_map/reduce_scatter | solution.py:182
  617.6 311.6 %reduce-scatter.25.cloned.1.call-start = ((), (), s32[]{:S(2)}) async-start(), calls=%async_computation.22 | async-start | bytes 5242880 | tf_op jit(solution)/shard_map/reduce_scatter | solution.py:182
  621.3 387.5 %reduce-scatter.35.cloned.1.call-start = ((), (), s32[]{:S(2)}) async-start(), calls=%async_computation.27 | async-start | bytes 5242880 | tf_op jit(solution)/shard_map/reduce_scatter | solution.py:182
  626.1 462.2 %reduce-scatter.29.cloned.1.call-start = ((), (), s32[]{:S(2)}) async-start(), calls=%async_computation.24 | async-start | bytes 5242880 | tf_op jit(solution)/shard_map/reduce_scatter | solution.py:182
  629.8 538.1 %reduce-scatter.27.cloned.1.call-start = ((), (), s32[]{:S(2)}) async-start(), calls=%async_computation.23 | async-start | bytes 5242880 | tf_op jit(solution)/shard_map/reduce_scatter | solution.py:182
  633.5 614.0 %reduce-scatter.23.cloned.1.call-start = ((), (), s32[]{:S(2)}) async-start(), calls=%async_computation.21 | async-start | bytes 5242880 | tf_op jit(solution)/shard_map/reduce_scatter | solution.py:182
  637.2 110.2 %copy-start.17 = (f32[256,1024]{1,0:T(8,128)S(1)}, f32[256,1024]{1,0:T(8,128)}, u32[]{:S(2)}) copy-start(f32[256,1024]{1,0:T(8,128)} %param.29) | copy-start | bytes 3145732
  637.2 689.8 %reduce-scatter.21.cloned.1.call-start = ((), (), s32[]{:S(2)}) async-start(), calls=%async_computation.20 | async-start | bytes 5242880 | tf_op jit(solution)/shard_map/reduce_scatter | solution.py:182
  641.2 749.8 %reduce-scatter.19.cloned.1.call-start = ((), (), s32[]{:S(2)}) async-start(), calls=%async_computation.18 | async-start | bytes 1351680 | tf_op jit(solution)/shard_map/reduce_scatter | solution.py:177
  747.5 579.6 %copy-start.48 = (bf16[256,261]{0,1:T(8,128)(2,1)}, bf16[256,261]{0,1:T(8,128)(2,1)S(1)}, u32[]{:S(2)}) copy-start(bf16[256,261]{0,1:T(8,128)(2,1)S(1)} %get-tuple-element.75) | copy-start | bytes 400900
  748.8 742.0 %all-reduce.9.cloned.1.call-start = ((), (), s32[]{:S(2)}) async-start(), calls=%async_computation.28 | async-start | bytes 16777216 | tf_op jit(solution)/shard_map/psum | solution.py:182
  (79 other events, 782.2 us)
Sparse Core Ops, SparseCore 0:
  18.5 332.9 all-gather.2
  361.6 35.7 all-gather.4
  460.7 71.2 reduce-scatter.12
  571.7 35.9 reduce-scatter.14
  610.0 52.8 all-reduce.6
  665.0 27.0 reduce-scatter.16
  694.4 75.4 reduce-scatter.32
  772.3 77.2 reduce-scatter.30
  851.9 77.2 reduce-scatter.24
  931.4 77.2 reduce-scatter.34
  1011.0 77.2 reduce-scatter.28
  1090.6 77.2 reduce-scatter.26
  1170.2 77.2 reduce-scatter.22
  1249.7 77.2 reduce-scatter.20
  1329.8 28.1 reduce-scatter.18
  1362.3 128.4 all-reduce.8
